TPU v7x, 32 devices: a whole 2x2x4 slice. The times are simulated.
32 devices in a mesh: dp: 8 (over y, x, core), tensor: 4 (over z).
Axes of the slice: x: 2, y: 2, z: 4, core: 2. Of those that a mesh axis runs over, the one named last changes fastest.
Arguments:
- x_in: bfloat16 [8192, 8192], P(('dp', 'tensor')), may hold values from -6 to 6
- z_in: bfloat16 [8192, 8192], P(('dp', 'tensor')), may hold values from -6 to 6
- bc_in: bfloat16 [8192, 2048], P(('dp', 'tensor')), may hold values from -6 to 6
- dt_in: bfloat16 [8192, 128], P(('dp', 'tensor')), may hold values from -4 to 4
- conv_x_param: float32 [5, 8192], P(None, 'tensor'), may hold values from -3 to 3
- conv_bc_param: float32 [5, 2048], P(None, 'tensor'), may hold values from -3 to 3
- decay_rate: float32 [128], P('tensor'), may hold values from 0.01 to 2
- dt_bias: float32 [128], P('tensor'), may hold values from -3 to 0
- skip_gain: float32 [128], P('tensor'), may hold values from -3 to 3
- norm_gain: float32 [8192], P('tensor'), may hold values from 0.5 to 1.5
- ssm_state: float32 [32, 128, 64, 128], P('dp', 'tensor'), may hold values from -0.6 to 0.6
- conv_x_state: float32 [32, 3, 8192], P('dp', None, 'tensor'), may hold values from -6 to 6
- conv_bc_state: float32 [32, 3, 2048], P('dp', None, 'tensor'), may hold values from -6 to 6
- lengths: int32 [32], replicated, may hold values from 3 to 640, as said below
- prefill_owner: int32 [32], replicated, may hold values from 0 to 7, as said below
- row_start: int32 [32], replicated, may hold values from 0 to 1021, as said below
Outputs:
- y_out: bfloat16 [8192, 8192], P('dp', 'tensor')
- new_ssm_state: float32 [32, 128, 64, 128], P('dp', 'tensor')
- new_conv_x_state: float32 [32, 3, 8192], P('dp', None, 'tensor')
- new_conv_bc_state: float32 [32, 3, 2048], P('dp', None, 'tensor')
Inputs may be any that keep to these rules, and one draw needn't show every extreme that they name: `prefill_owner`: conversation c is held by index c // 4 along dp. Of the 4 conversations of one index, two are prefilled there, one on the next index and one on the previous index, cyclically; so every index prefills 4 conversations. The lengths of the conversations of one prefill owner add up to 1024. `row_start`: the conversations of one prefill owner cover its 1024 rows in consecutive runs, each row in exactly one.
All inputs are finite; a program needn't handle non-finite values.
Results may differ from a plain program's by a relative error of at most 0.005.
Values may be sent and summed in bfloat16 or wider, within the bound.
A program may use at most 128 MiB of HBM per device.

v0:
```python
import jax
import jax.numpy as jnp
from jax import lax
from jax.sharding import PartitionSpec as P

HEADS = 128
HEADDIM = 64
STATE = 128
GROUPS = 8
SLOTS = 4


EPSILON = 1e-05
best_precision = lax.Precision.HIGHEST


def shifted_2(value, axis, steps):
    count = lax.axis_size(axis)
    pairs = [(source, (source + steps) % count) for source in range(count)]
    return lax.ppermute(value, axis, pairs)


def shortened(array):

    def short(part):
        return part.astype(jnp.bfloat16) if part.dtype == jnp.float32 else part

    return jax.tree.map(short, array)


def plan_rows(owner_idx, lengths, prefill_owner, row_start, row_count):
    conv_ids = jnp.nonzero(prefill_owner == owner_idx, size=SLOTS)[0].astype(jnp.int32)
    order_idx = jnp.argsort(row_start[conv_ids])
    conv_ids = conv_ids[order_idx]
    starts = row_start[conv_ids]
    seg_lengths = lengths[conv_ids]
    row_idx = jnp.arange(row_count, dtype=jnp.int32)
    inside = (row_idx[:, None] >= starts[None, :]) & (
        row_idx[:, None] < (starts + seg_lengths)[None, :]
    )
    segment = jnp.sum(jnp.where(inside, jnp.arange(SLOTS, dtype=jnp.int32)[None, :], 0), axis=1)
    position = row_idx - jnp.sum(jnp.where(inside, starts[None, :], 0), axis=1)
    same_tri = (segment[:, None] == segment[None, :]) & (row_idx[None, :] <= row_idx[:, None])
    return (conv_ids, starts, seg_lengths, inside, position, same_tri)


def causal_conv(values, param, state, inside, position):
    row_count, channels = values.shape
    result = param[4][None, :] + param[3][None, :] * values
    for lag_rows in (1, 2, 3):
        shifted = jnp.concatenate(
            [jnp.zeros((lag_rows, channels), jnp.float32), values[:-lag_rows]], axis=0
        )
        picker = inside[:, :, None] & (
            (3 - lag_rows + position)[:, None, None]
            == jnp.arange(3, dtype=jnp.int32)[None, None, :]
        )
        from_state = jnp.dot(
            picker.astype(jnp.float32).reshape(row_count, SLOTS * 3),
            state.reshape(SLOTS * 3, channels),
            precision=best_precision,
            preferred_element_type=jnp.float32,
        )
        previous = jnp.where((position >= lag_rows)[:, None], shifted, from_state)
        result = result + param[3 - lag_rows][None, :] * previous
    return result


def last_inputs(values, starts, seg_lengths):
    row_idx = jnp.arange(values.shape[0], dtype=jnp.int32)
    target = (starts + seg_lengths)[:, None] - 3 + jnp.arange(3, dtype=jnp.int32)[None, :]
    picker = (
        (target[:, :, None] == row_idx[None, None, :])
        .astype(jnp.float32)
        .reshape(SLOTS * 3, values.shape[0])
    )
    taken = jnp.dot(picker, values, precision=best_precision, preferred_element_type=jnp.float32)
    return taken.reshape(SLOTS, 3, values.shape[1])


def head_scan(
    x_head,
    dt_head,
    decay_speed,
    skip_value,
    mix_matrix,
    c_half,
    b_half,
    initial_head,
    inside,
    starts,
    seg_lengths,
    same_tri,
):
    log_decay = -dt_head * decay_speed
    running = jnp.cumsum(log_decay)
    before = running[starts] - log_decay[starts]
    cumulated = running - jnp.sum(jnp.where(inside, before[None, :], 0.0), axis=1)
    end_decay = running[starts + seg_lengths - 1] - before
    spread = jnp.where(same_tri, cumulated[:, None] - cumulated[None, :], 0.0)
    decay_matrix = jnp.where(same_tri, jnp.exp(spread), 0.0)
    scores = (mix_matrix * decay_matrix * dt_head[None, :]).astype(jnp.bfloat16)
    output = jnp.dot(scores, x_head, preferred_element_type=jnp.float32)
    state_rows = jnp.transpose(initial_head, (2, 0, 1)).reshape(
        initial_head.shape[2], SLOTS * HEADDIM
    )
    state_hi = state_rows.astype(jnp.bfloat16)
    state_lo = (state_rows - lax.optimization_barrier(state_hi).astype(jnp.float32)).astype(
        jnp.bfloat16
    )
    initial_term = jnp.dot(c_half, state_hi, preferred_element_type=jnp.float32) + jnp.dot(
        c_half, state_lo, preferred_element_type=jnp.float32
    )
    initial_term = jnp.sum(
        jnp.where(inside[:, :, None], initial_term.reshape(-1, SLOTS, HEADDIM), 0.0), axis=1
    )
    x_wide = x_head.astype(jnp.float32)
    output = output + jnp.exp(cumulated)[:, None] * initial_term + skip_value * x_wide
    row_end = jnp.sum(jnp.where(inside, end_decay[None, :], 0.0), axis=1)
    carried = (x_wide * (jnp.exp(row_end - cumulated) * dt_head)[:, None]).astype(jnp.bfloat16)
    b_slots = jnp.where(
        inside[:, :, None], b_half[:, None, :], jnp.zeros((), jnp.bfloat16)
    ).reshape(b_half.shape[0], -1)
    final_state = jnp.dot(carried.T, b_slots, preferred_element_type=jnp.float32).reshape(
        HEADDIM, SLOTS, -1
    )
    final_state = (
        jnp.transpose(final_state, (1, 0, 2)) + jnp.exp(end_decay)[:, None, None] * initial_head
    )
    return (output, final_state)


def group_block(
    x_group,
    z_group,
    bc_group,
    dt_group,
    rate_group,
    skip_group,
    gain_group,
    initial_group,
    inside,
    starts,
    seg_lengths,
    same_tri,
):
    b_half = bc_group[:, :STATE]
    c_half = bc_group[:, STATE:]
    mix_matrix = jnp.dot(c_half, b_half.T, preferred_element_type=jnp.float32)

    def one_head(head_idx):
        x_head = lax.dynamic_slice_in_dim(x_group, head_idx * HEADDIM, HEADDIM, 1)
        dt_head = lax.dynamic_index_in_dim(dt_group, head_idx, 1, keepdims=False)
        decay_speed = lax.dynamic_index_in_dim(rate_group, head_idx, 0, keepdims=False)
        skip_value = lax.dynamic_index_in_dim(skip_group, head_idx, 0, keepdims=False)
        initial_head = lax.dynamic_index_in_dim(initial_group, head_idx, 1, keepdims=False)
        return head_scan(
            x_head,
            dt_head,
            decay_speed,
            skip_value,
            mix_matrix,
            c_half,
            b_half,
            initial_head,
            inside,
            starts,
            seg_lengths,
            same_tri,
        )

    head_outputs, head_states = lax.map(one_head, jnp.arange(HEADS // GROUPS, dtype=jnp.int32))
    joined = jnp.transpose(head_outputs, (1, 0, 2)).reshape(head_outputs.shape[1], -1)
    gated = joined * jax.nn.silu(z_group.astype(jnp.float32))
    mean_square = jnp.mean(gated * gated, axis=1, keepdims=True)
    normed = (gated * lax.rsqrt(mean_square + EPSILON) * gain_group[None, :]).astype(jnp.bfloat16)
    return (normed, jnp.transpose(head_states, (1, 0, 2, 3)))


def mixer(
    x_rows,
    z_rows,
    bc_rows,
    dt_rows,
    conv_x_param,
    conv_bc_param,
    decay_rate,
    dt_bias,
    skip_gain,
    norm_gain,
    initial_ssm,
    initial_cx,
    initial_cbc,
    inside,
    position,
    starts,
    seg_lengths,
    same_tri,
):
    x_values = x_rows.astype(jnp.float32)
    bc_values = bc_rows.astype(jnp.float32)
    x_conv = jax.nn.silu(causal_conv(x_values, conv_x_param, initial_cx, inside, position)).astype(
        jnp.bfloat16
    )
    bc_conv = jax.nn.silu(
        causal_conv(bc_values, conv_bc_param, initial_cbc, inside, position)
    ).astype(jnp.bfloat16)
    dt_all = jax.nn.softplus(dt_rows.astype(jnp.float32) + dt_bias[None, :])
    per_group = HEADS // GROUPS
    group_count = dt_rows.shape[1] // per_group
    outputs = []
    finals = []
    for group_idx in range(group_count):
        col_lo = group_idx * per_group * HEADDIM
        col_hi = col_lo + per_group * HEADDIM
        head_lo = group_idx * per_group
        head_hi = head_lo + per_group
        bc_lo = group_idx * 2 * STATE
        normed, final_group = group_block(
            x_conv[:, col_lo:col_hi],
            z_rows[:, col_lo:col_hi],
            bc_conv[:, bc_lo : bc_lo + 2 * STATE],
            dt_all[:, head_lo:head_hi],
            decay_rate[head_lo:head_hi],
            skip_gain[head_lo:head_hi],
            norm_gain[col_lo:col_hi],
            initial_ssm[:, head_lo:head_hi],
            inside,
            starts,
            seg_lengths,
            same_tri,
        )
        outputs.append(normed)
        finals.append(final_group)
    y_block = jnp.concatenate(outputs, axis=1)
    final_ssm = jnp.concatenate(finals, axis=1)
    return (
        y_block,
        final_ssm,
        last_inputs(x_values, starts, seg_lengths),
        last_inputs(bc_values, starts, seg_lengths),
    )


def select_slots(wanted, groups):
    combined = None
    for arrays, known in groups:
        match = (wanted[:, None] == known[None, :]).astype(jnp.float32)
        part_sum = tuple(
            (jnp.tensordot(match, piece, axes=1, precision=best_precision) for piece in arrays)
        )
        if combined is None:
            combined = part_sum
        else:
            combined = tuple(
                (old_part + new_part for old_part, new_part in zip(combined, part_sum))
            )
    return combined


def shards(
    x_in,
    z_in,
    bc_in,
    dt_in,
    conv_x_param,
    conv_bc_param,
    decay_rate,
    dt_bias,
    skip_gain,
    norm_gain,
    ssm_state,
    conv_x_state,
    conv_bc_state,
    lengths,
    prefill_owner,
    row_start,
):
    x_rows, z_rows, bc_rows, dt_rows = (
        lax.all_to_all(x_in, "tensor", split_axis=1, concat_axis=0, tiled=True),
        lax.all_to_all(z_in, "tensor", split_axis=1, concat_axis=0, tiled=True),
        lax.all_to_all(bc_in, "tensor", split_axis=1, concat_axis=0, tiled=True),
        lax.all_to_all(dt_in, "tensor", split_axis=1, concat_axis=0, tiled=True),
    )
    dp_count = lax.axis_size("dp")
    my_index = lax.axis_index("dp")
    left_index = (my_index + dp_count - 1) % dp_count
    right_index = (my_index + 1) % dp_count
    slot_iota = jnp.arange(SLOTS, dtype=jnp.int32)
    own_ids = my_index * SLOTS + slot_iota
    my_dest = lax.dynamic_slice_in_dim(prefill_owner, my_index * SLOTS, SLOTS)
    right_slot = jnp.sum(jnp.where(my_dest == right_index, slot_iota, 0))
    left_slot = jnp.sum(jnp.where(my_dest == left_index, slot_iota, 0))
    right_mover = my_index * SLOTS + right_slot
    left_mover = my_index * SLOTS + left_slot
    from_left = shifted_2((ssm_state, conv_x_state, conv_bc_state), "dp", 1)
    from_right = shifted_2((ssm_state, conv_x_state, conv_bc_state), "dp", -1)
    left_ids = left_index * SLOTS + slot_iota
    right_ids = right_index * SLOTS + slot_iota
    row_count = x_rows.shape[0]
    conv_ids, starts, seg_lengths, inside, position, same_tri = plan_rows(
        my_index, lengths, prefill_owner, row_start, row_count
    )
    initial_ssm, initial_cx, initial_cbc = select_slots(
        conv_ids,
        [
            ((ssm_state, conv_x_state, conv_bc_state), own_ids),
            (from_left, left_ids),
            (from_right, right_ids),
        ],
    )
    y_out, final_ssm, final_cx, final_cbc = mixer(
        x_rows,
        z_rows,
        bc_rows,
        dt_rows,
        conv_x_param,
        conv_bc_param,
        decay_rate,
        dt_bias,
        skip_gain,
        norm_gain,
        initial_ssm,
        initial_cx,
        initial_cbc,
        inside,
        position,
        starts,
        seg_lengths,
        same_tri,
    )
    finals = (final_ssm, final_cx, final_cbc)
    came_left = jnp.sum(jnp.where(conv_ids // SLOTS == left_index, conv_ids, 0))[None]
    came_right = jnp.sum(jnp.where(conv_ids // SLOTS == right_index, conv_ids, 0))[None]
    back_ssm_l, back_cx_l, back_cbc_l = select_slots(came_left, [(finals, conv_ids)])
    back_ssm_r, back_cx_r, back_cbc_r = select_slots(came_right, [(finals, conv_ids)])
    returned_from_right = (
        shifted_2(shortened(back_ssm_l), "dp", -1).astype(back_ssm_l.dtype),
        shifted_2(shortened(back_cx_l), "dp", -1).astype(back_cx_l.dtype),
        shifted_2(shortened(back_cbc_l), "dp", -1).astype(back_cbc_l.dtype),
    )
    returned_from_left = (
        shifted_2(shortened(back_ssm_r), "dp", 1).astype(back_ssm_r.dtype),
        shifted_2(shortened(back_cx_r), "dp", 1).astype(back_cx_r.dtype),
        shifted_2(shortened(back_cbc_r), "dp", 1).astype(back_cbc_r.dtype),
    )
    new_ssm, new_cx, new_cbc = select_slots(
        own_ids,
        [
            (finals, conv_ids),
            (returned_from_right, right_mover[None]),
            (returned_from_left, left_mover[None]),
        ],
    )
    return (y_out, new_ssm, new_cx, new_cbc)


def solution(mesh):
    in_specs = (
        P(("dp", "tensor"), None),
        P(("dp", "tensor"), None),
        P(("dp", "tensor"), None),
        P(("dp", "tensor"), None),
        P(None, "tensor"),
        P(None, "tensor"),
        P("tensor"),
        P("tensor"),
        P("tensor"),
        P("tensor"),
        P("dp", "tensor", None, None),
        P("dp", None, "tensor"),
        P("dp", None, "tensor"),
        P(),
        P(),
        P(),
    )
    out_specs = (
        P("dp", "tensor"),
        P("dp", "tensor", None, None),
        P("dp", None, "tensor"),
        P("dp", None, "tensor"),
    )
    return jax.shard_map(shards, mesh=mesh, in_specs=in_specs, out_specs=out_specs, check_vma=False)
```

profile of v0, /device:TPU:0, one launch (start us, length us, event | category | flops | bytes accessed | tf_op | source)
XLA Modules:
  0.0 853.1 jit_solution(3416875460832039905)
XLA Ops:
  4.2 7.8 copy.81
  15.3 5.6 all-to-all-start
  29.3 10.6 %fusion.117 = f32[4,32,64,128]{3,0,2,1:T(4,128)} fusion(s32[4]{0:T(128)S(1)} %iota_add_fusion.3, s32[4]{0:T(128)S(1)} %gather_fusion.7, f32[4,32,64,128]{3,2,1,0:T(8,128)} %param.30), kind=kOutput, calls=%fused_computation.254 | convolution fusion | flops 50331664 | bytes 8388640 | tf_op jit(solution)/shard_map/dot_general | solution.py:250
  47.6 5.1 all-to-all-start.1
  57.5 6.4 copy.87
  63.8 40.9 %collective-permute-done = f32[4,3,512]{2,0,1:T(4,128)S(1)} collective-permute-done((f32[4,3,512]{2,0,1:T(4,128)S(1)}, f32[4,3,512]{2,0,1:T(4,128)S(1)}, u32[]{:S(2)}, u32[]{:S(2)}) %collective-permute-start) | collective-permute-done | bytes 24608 | tf_op jit(solution)/shard_map/ppermute | solution.py:20
  111.1 6.6 all-to-all-start.2
  119.7 5.8 fusion.84
  125.5 5.8 fusion.88
  150.6 6.5 fusion.118
  157.1 7.3 add_add_fusion
  166.7 44.4 %all-to-all-done.2 = bf16[256,4,2048]{2,0,1:T(8,128)(2,1)} async-done(((bf16[256,4,2048]{2,0,1:T(8,128)(2,1)}), bf16[256,4,2048]{2,0,1:T(8,128)(2,1)}, u32[]{:S(2)}, u32[]{:S(2)}) %all-to-all-start.2) | async-done | bytes 4194336 | tf_op jit(solution)/shard_map/all_to_all | solution.py:280
  211.1 5.1 all-to-all-start.3
  219.5 16.2 %multiply_convert_fusion.20 = bf16[1024,2048]{1,0:T(8,128)(2,1)S(1)} fusion(f32[1024,2048,1]{1,0,2:T(8,128)} %fusion.84, f32[1024,2048,1]{1,0,2:T(8,128)} %fusion.88, f32[1021,2048]{1,0:T(8,128)S(1)} %bitcast.510, f32[1022,2048]{1,0:T(8,128)S(1)} %bitcast.511, f32[1023,2048]{1,0:T(8,128)S(1)} %bitcast.512, f32[1024,2048]{1,0:T(8,128)S(1)} %bitcast_convert_fusion.2, ...), kind=kOutput, calls=%fused_computation.130 | convolution fusion | flops 335556608 | bytes 54626304 | tf_op jit(solution)/shard_map/dot_general | solution.py:58
  245.9 281.6 %while.37 = (s32[]{:T(128)}, f32[16,1024,64]{1,2,0:T(8,128)}, f32[16,4,64,128]{3,1,2,0:T(4,128)}, s32[16]{0:T(128)S(1)}, f32[1024,16]{0,1:T(8,128)}, /*index=5*/...) while((s32[]{:T(128)}, f32[16,1024,64]{1,2,0:T(8,128)}, ...), condition=%wide.region_21.22_spmd.clone.clone, body=%wide.region_15.21_spmd.clone.clone.sunk | while | flops 347117664 | bytes 12135961 | solution.py:172
  533.0 263.8 %while.36 = (s32[]{:T(128)}, f32[16,1024,64]{1,2,0:T(8,128)}, f32[16,4,64,128]{3,1,2,0:T(4,128)S(1)}, s32[16]{0:T(128)S(1)}, f32[1024,16]{0,1:T(8,128)S(1)}, /*i...) while((s32[]{:T(128)}, f32[16,1024,64]{1,2,0:T(8,128)}, ...), condition=%wide.region_13.14_spmd.clone.clone, body=%wide.region_7.13_spmd.clone.clone.sunk | while | flops 347117664 | bytes 12135453 | solution.py:172
  542.9 5.0 fusion.257
  559.4 5.0 fusion.257
  575.9 5.0 fusion.257
  592.3 5.0 fusion.257
  608.8 5.0 fusion.257
  625.3 5.0 fusion.257
  829.7 6.4 copy.94
  842.4 7.9 multiply_add_fusion
  (1212 shorter events, 550.8 us)
Async XLA Ops:
  0.6 23.6 %copy-start = (s32[32]{0:T(128)S(1)}, s32[32]{0:T(128)}, u32[]{:S(2)}) copy-start(s32[32]{0:T(128)} %param.35) | copy-start | bytes 388
  0.6 28.3 %copy-start.10 = (f32[4,3,2048]{2,0,1:T(4,128)S(1)}, f32[4,3,2048]{2,0,1:T(4,128)}, u32[]{:S(2)}) copy-start(f32[4,3,2048]{2,0,1:T(4,128)} %param.31) | copy-start | bytes 294916
  0.7 20.2 %copy-start.43 = (s32[32]{0:T(128)S(1)}, s32[32]{0:T(128)}, u32[]{:S(2)}) copy-start(s32[32]{0:T(128)} %param.34) | copy-start | bytes 388
  0.7 26.3 %copy-start.2 = (s32[32]{0:T(128)S(1)}, s32[32]{0:T(128)}, u32[]{:S(2)}) copy-start(s32[32]{0:T(128)} %param.33) | copy-start | bytes 388
  0.7 109.2 %collective-permute-start.2 = (f32[4,3,2048]{2,0,1:T(4,128)}, f32[4,3,2048]{2,0,1:T(4,128)}, u32[]{:S(2)}, u32[]{:S(2)}) collective-permute-start(f32[4,3,2048]{2,0,1:T(4,128)} %param.31), channel_id=1, source_target_pairs={{0,4},{4,8},{8,12},{12,16},{16,20},{20,24},{24,28},{28,0},{1,5},{5... | collective-permute-start | bytes 294920 | tf_op jit(solution)/shard_map/ppermute | solution.py:20
  1.2 117.3 %collective-permute-start.3 = (f32[4,3,2048]{2,0,1:T(4,128)}, f32[4,3,2048]{2,0,1:T(4,128)}, u32[]{:S(2)}, u32[]{:S(2)}) collective-permute-start(f32[4,3,2048]{2,0,1:T(4,128)} %param.31), channel_id=1, source_target_pairs={{0,28},{4,0},{8,4},{12,8},{16,12},{20,16},{24,20},{28,24},{1,29},{... | collective-permute-start | bytes 294920 | tf_op jit(solution)/shard_map/ppermute | solution.py:20
  11.9 138.7 %collective-permute-start.4 = (f32[4,32,64,128]{3,0,2,1:T(4,128)}, f32[4,32,64,128]{3,0,2,1:T(4,128)}, u32[]{:S(2)}, u32[]{:S(2)}) collective-permute-start(f32[4,32,64,128]{3,0,2,1:T(4,128)} %copy.81), channel_id=1, source_target_pairs={{0,4},{4,8},{8,12},{12,16},{16,20},{20,24},{24,28},{28,0},{1,5},{5... | collective-permute-start | bytes 12582920 | tf_op jit(solution)/shard_map/ppermute | solution.py:20
  11.9 145.1 %collective-permute-start.5 = (f32[4,32,64,128]{3,0,2,1:T(4,128)}, f32[4,32,64,128]{3,0,2,1:T(4,128)}, u32[]{:S(2)}, u32[]{:S(2)}) collective-permute-start(f32[4,32,64,128]{3,0,2,1:T(4,128)} %copy.81), channel_id=1, source_target_pairs={{0,28},{4,0},{8,4},{12,8},{16,12},{20,16},{24,20},{28,24},{1,29},{... | collective-permute-start | bytes 12582920 | tf_op jit(solution)/shard_map/ppermute | solution.py:20
  14.6 90.2 %collective-permute-start = (f32[4,3,512]{2,0,1:T(4,128)S(1)}, f32[4,3,512]{2,0,1:T(4,128)S(1)}, u32[]{:S(2)}, u32[]{:S(2)}) collective-permute-start(f32[4,3,512]{2,0,1:T(4,128)S(1)} %copy-done.48), channel_id=1, source_target_pairs={{0,4},{4,8},{8,12},{12,16},{16,20},{20,24},{24,28},{28,0},{1,5},{5... | collective-permute-start | bytes 73736 | tf_op jit(solution)/shard_map/ppermute | solution.py:20
  15.3 32.3 %all-to-all-start = ((bf16[256,4,32]{0,2,1:T(8,128)(2,1)}), bf16[256,4,32]{0,2,1:T(8,128)(2,1)S(1)}, u32[]{:S(2)}, u32[]{:S(2)}) async-start(bf16[256,4,32]{0,2,1:T(8,128)(2,1)} %bitcast), calls=%async_computation | async-start | bytes 131072 | tf_op jit(solution)/shard_map/all_to_all | solution.py:283
  29.3 17.1 %copy-start.37 = (f32[32]{0:T(128)S(1)}, f32[32]{0:T(128)}, u32[]{:S(2)}) copy-start(f32[32]{0:T(128)} %param.28) | copy-start | bytes 388
  29.3 17.1 %copy-start.38 = (f32[32]{0:T(128)S(1)}, f32[32]{0:T(128)}, u32[]{:S(2)}) copy-start(f32[32]{0:T(128)} %param.26) | copy-start | bytes 388
  47.6 57.1 %copy-start.23 = (s32[4]{0:T(128)}, s32[4]{0:T(128)S(1)}, u32[]{:S(2)}) copy-start(s32[4]{0:T(128)S(1)} %iota_add_fusion.2) | copy-start | bytes 52
  47.6 63.5 %all-to-all-start.1 = ((bf16[256,4,512]{2,0,1:T(8,128)(2,1)}), bf16[256,4,512]{2,0,1:T(8,128)(2,1)S(1)}, u32[]{:S(2)}, u32[]{:S(2)}) async-start(bf16[256,4,512]{2,0,1:T(8,128)(2,1)} %bitcast.386), calls=%async_computation.1 | async-start | bytes 2097152 | tf_op jit(solution)/shard_map/all_to_all | solution.py:282
  52.7 53.5 %copy-start.26 = (s32[4]{0:T(128)}, s32[4]{0:T(128)S(1)}, u32[]{:S(2)}) copy-start(s32[4]{0:T(128)S(1)} %iota_add_fusion.1) | copy-start | bytes 52
  104.7 1.5 collective-permute-start.1
  111.1 100.0 %all-to-all-start.2 = ((bf16[256,4,2048]{2,0,1:T(8,128)(2,1)}), bf16[256,4,2048]{2,0,1:T(8,128)(2,1)}, u32[]{:S(2)}, u32[]{:S(2)}) async-start(bf16[256,4,2048]{2,0,1:T(8,128)(2,1)} %bitcast.508), calls=%async_computation.2 | async-start | bytes 8388608 | tf_op jit(solution)/shard_map/all_to_all | solution.py:280
  132.7 15.7 %collective-permute-start.11 = (bf16[1,3,512]{2,1,0:T(4,128)(2,1)S(1)}, bf16[1,3,512]{2,1,0:T(4,128)(2,1)S(1)}, u32[]{:S(2)}, u32[]{:S(2)}) collective-permute-start(bf16[1,3,512]{2,1,0:T(4,128)(2,1)S(1)} %copy.147), channel_id=1, source_target_pairs={{0,4},{4,8},{8,12},{12,16},{16,20},{20,24},{24,28},{28,0},{1,5},{5... | collective-permute-start | bytes 9224 | tf_op jit(solution)/shard_map/ppermute | solution.py:20
  145.4 4.3 collective-permute-start.10
  211.1 604.5 %all-to-all-start.3 = ((bf16[256,4,2048]{0,2,1:T(8,128)(2,1)}), bf16[256,4,2048]{0,2,1:T(8,128)(2,1)}, u32[]{:S(2)}, u32[]{:S(2)}) async-start(bf16[256,4,2048]{0,2,1:T(8,128)(2,1)} %bitcast.507), calls=%async_computation.3 | async-start | bytes 8388608 | tf_op jit(solution)/shard_map/all_to_all | solution.py:281
  804.7 36.3 %collective-permute-start.6 = (bf16[1,32,64,128]{3,2,1,0:T(8,128)(2,1)S(1)}, bf16[1,32,64,128]{3,2,1,0:T(8,128)(2,1)S(1)}, u32[]{:S(2)}, u32[]{:S(2)}) collective-permute-start(bf16[1,32,64,128]{3,2,1,0:T(8,128)(2,1)S(1)} %convert_bitcast_fusion.1), channel_id=1, source_target_pairs={{0,28},{4,0},{8,4},{12,8},{16,12},{20,16},{24,20},{28,24},{1,29},{... | collective-permute-start | bytes 1572872 | tf_op jit(solution)/shard_map/ppermute | solution.py:20
  810.5 30.7 %collective-permute-start.7 = (bf16[1,32,64,128]{3,2,1,0:T(8,128)(2,1)}, bf16[1,32,64,128]{3,2,1,0:T(8,128)(2,1)}, u32[]{:S(2)}, u32[]{:S(2)}) collective-permute-start(bf16[1,32,64,128]{3,2,1,0:T(8,128)(2,1)} %convert_bitcast_fusion), channel_id=1, source_target_pairs={{0,4},{4,8},{8,12},{12,16},{16,20},{20,24},{24,28},{28,0},{1,5},{5... | collective-permute-start | bytes 1572872 | tf_op jit(solution)/shard_map/ppermute | solution.py:20
  823.7 15.0 %collective-permute-start.9 = (bf16[1,3,2048]{2,1,0:T(4,128)(2,1)S(1)}, bf16[1,3,2048]{2,1,0:T(4,128)(2,1)S(1)}, u32[]{:S(2)}, u32[]{:S(2)}) collective-permute-start(bf16[1,3,2048]{2,1,0:T(4,128)(2,1)S(1)} %copy.145), channel_id=1, source_target_pairs={{0,4},{4,8},{8,12},{12,16},{16,20},{20,24},{24,28},{28,0},{1,5},{5... | collective-permute-start | bytes 36872 | tf_op jit(solution)/shard_map/ppermute | solution.py:20
  836.1 4.0 collective-permute-start.8
  (41 other events, 268.6 us)
where the time goes:
time: 864 us; the launch traced here: 853 us
  matrix products  315 us (36%)
  local copies, waits for them, and re-layouts  226 us (26%)
  other arithmetic  103 us (12%)
  waiting for transfers between devices  89.4 us (10%)
  loops' own time  80.9 us (9%)
  starting transfers between devices  34.8 us (4%)
    dot_general x32, matrix products, head_scan(): output = jnp.dot(scores, x_head, preferred_element_type=jnp.float32)  159 us
    another operation x2, loops' own time, group_block(): lax.map(one_head, jnp.arange(HEADS // GROUPS, dtype=jnp.int32))  80.9 us
    mul x64, other arithmetic, head_scan(): log_decay = -dt_head * decay_speed  50.8 us
    ppermute x12, waiting for transfers between devices, shifted_2(): return lax.ppermute(value, axis, pairs)  45 us
    all_to_all x1, waiting for transfers between devices, shards(): lax.all_to_all(x_in, 'tensor', split_axis=1, concat_axis=0, tiled=True)  44.4 us
    dot_general x32, matrix products, head_scan(): jnp.dot(carried.T, b_slots, preferred_element_type=jnp.float32)  43.5 us
    dot_general x16, matrix products, select_slots(): jnp.tensordot(match, piece, axes=1, precision=best_precision)  40.6 us
    gather x64, local copies, waits for them, and re-layouts, head_scan(): before = running[starts] - log_decay[starts]  40.2 us
  transfers between devices with their start and end apart: 16, of which 5 were waited for; matrix products, arithmetic and copies ran while one was open for 74% of the time, Pallas kernels for 0%

commit v1 on v0

v1 whole, which is shorter than its diff:
```python
import functools

import jax
import jax.numpy as jnp
from jax import lax
from jax.experimental import pallas as pl
from jax.experimental.pallas import tpu as pltpu
from jax.sharding import PartitionSpec as P

HEADS = 128
HEADDIM = 64
STATE = 128
GROUPS = 8
SLOTS = 4
PER_GROUP = HEADS // GROUPS
WIDTH = PER_GROUP * HEADDIM
CHUNK = 256
LANES = 128
EPSILON = 1e-05
LOG2E = 1.4426950408889634
F32 = jnp.float32
BF16 = jnp.bfloat16
best_precision = lax.Precision.HIGHEST


def silu(value):
    half = 0.5 * value
    return half + half * jnp.tanh(half)


def parts_of(value, count):
    parts = []
    for _ in range(count):
        part = value.astype(BF16)
        parts.append(part)
        value = value - part.astype(F32)
    return jnp.concatenate(parts, axis=-1)


def dot(a, b):
    return jnp.dot(a, b, preferred_element_type=F32)


def scan_kernel(
    idx_ref,
    x_ref,
    bc_ref,
    dt_ref,
    log_ref,
    segc_ref,
    segr_ref,
    pos_ref,
    pick_ref,
    fix_x_ref,
    fix_bc_ref,
    par_x_ref,
    par_bc_ref,
    skip_ref,
    spread_ref,
    init0,
    init1,
    init2,
    init3,
    y_ref,
    fin_ref,
    state,
    xs,
    bs,
    xb,
    inter,
):
    chunk = pl.program_id(1)
    inits = (init0, init1, init2, init3)

    @pl.when(chunk == 0)
    def _():
        for k in range(SLOTS):
            state[k * STATE : (k + 1) * STATE, :] = inits[k][0].T
        xs[0:8, :] = jnp.zeros((8, xs.shape[1]), F32)
        bs[0:8, :] = jnp.zeros((8, bs.shape[1]), F32)

    @pl.when(chunk > 0)
    def _():
        xs[0:8, :] = xs[CHUNK : CHUNK + 8, :]
        bs[0:8, :] = bs[CHUNK : CHUNK + 8, :]

    xs[8 : CHUNK + 8, :] = x_ref[...].astype(F32)
    bs[8 : CHUNK + 8, :] = bc_ref[...].astype(F32)
    pos = pos_ref[...]
    pick = pick_ref[...]

    def conv(src, par_ref, fix_ref, lo):
        cols = slice(lo, lo + LANES)
        total = dot(pick, fix_ref[:, cols]) + par_ref[4:5, cols]
        total = total + par_ref[3:4, cols] * src[8 : CHUNK + 8, cols]
        for lag in (1, 2, 3):
            before = jnp.where(pos >= lag, src[8 - lag : CHUNK + 8 - lag, cols], 0.0)
            total = total + par_ref[3 - lag : 4 - lag, cols] * before
        return silu(total)

    for lo in range(0, WIDTH, LANES):
        xb[:, lo : lo + LANES] = conv(xs, par_x_ref, fix_x_ref, lo).astype(BF16)
    b_half = conv(bs, par_bc_ref, fix_bc_ref, 0).astype(BF16)
    c_half = conv(bs, par_bc_ref, fix_bc_ref, STATE).astype(BF16)
    b_wide = b_half.astype(F32)
    c_wide = c_half.astype(F32)

    segc = segc_ref[...]
    segr = segr_ref[0:1, :]
    same = jnp.concatenate([segc, segc], axis=1) == segr
    row = lax.broadcasted_iota(jnp.int32, (CHUNK, CHUNK), 0)
    col = lax.broadcasted_iota(jnp.int32, (CHUNK, CHUNK), 1)
    tri = same & (col <= row)
    upto = jnp.where(tri, 1.0, 0.0).astype(BF16)
    after = jnp.where(same & (col > row), 1.0, 0.0).astype(BF16)
    slot = lax.broadcasted_iota(jnp.int32, (8, CHUNK), 0).astype(F32)
    owned = jnp.where(slot == segr, 1.0, 0.0).astype(BF16)

    logs = parts_of(log_ref[0], 3)

    def summed(mask):
        three = dot(mask, logs)
        return three[:, :LANES] + three[:, LANES : 2 * LANES] + three[:, 2 * LANES :]

    spread = spread_ref[...]

    def expanded(value):
        return dot(parts_of(value, 2), spread)

    dt = dt_ref[0]
    grown = summed(upto)
    back = (grown - jnp.log2(dt)).T
    into = expanded(jnp.exp2(summed(after)) * dt)
    keep = expanded(jnp.exp2(summed(owned)))

    mix = lax.dot_general(c_half, b_half, (((1,), (1,)), ((), ())), preferred_element_type=F32)
    mix = jnp.where(tri, mix, 0.0)
    c_slots = jnp.concatenate(
        [jnp.where(segc == k, c_wide, 0.0).astype(BF16) for k in range(SLOTS)], axis=1
    )
    inter[...] = dot(c_slots, state[...].astype(BF16)) * expanded(jnp.exp2(grown))

    b_turned = b_wide.T
    b_slots = jnp.concatenate(
        [jnp.where(segr == k, b_turned, 0.0).astype(BF16) for k in range(SLOTS)], axis=0
    )
    carried = (xb[...].astype(F32) * into).astype(BF16)
    update = dot(b_slots, carried)
    for k in range(SLOTS):
        rows = slice(k * STATE, (k + 1) * STATE)
        state[rows, :] = state[rows, :] * keep[k : k + 1, :] + update[rows, :]

    left_lanes = lax.broadcasted_iota(jnp.int32, (CHUNK, LANES), 1) < HEADDIM
    for pair in range(PER_GROUP // 2):
        cols = slice(pair * LANES, (pair + 1) * LANES)
        xp = xb[:, cols]
        both = []
        for h in (2 * pair, 2 * pair + 1):
            gap = jnp.minimum(grown[:, h : h + 1] - back[h : h + 1, :], 64.0)
            both.append(dot((mix * jnp.exp2(gap)).astype(BF16), xp))
        y = jnp.where(left_lanes, both[0], both[1])
        y_ref[:, cols] = y + inter[:, cols] + skip_ref[0:1, cols] * xp.astype(F32)

    @pl.when(chunk == pl.num_programs(1) - 1)
    def _():
        for k in range(SLOTS):
            fin_ref[k] = state[k * STATE : (k + 1) * STATE, :].T


def gate_kernel(y_ref, z_ref, gain_ref, out_ref):
    gated = y_ref[...] * silu(z_ref[...].astype(F32))
    square = jnp.mean(gated * gated, axis=1, keepdims=True)
    out_ref[...] = (gated * lax.rsqrt(square + EPSILON) * gain_ref[...]).astype(BF16)


def run_scan(idx, x_rows, bc_rows, dt, logs, segc, segr, pos, pick, fix_x, fix_bc, par_x, par_bc, skip, states):
    rows = x_rows.shape[0]
    groups = x_rows.shape[1] // WIDTH
    chunks = rows // CHUNK
    heads = jnp.arange(2 * LANES, dtype=jnp.int32)[:, None] % LANES
    spread = (heads == jnp.arange(WIDTH, dtype=jnp.int32)[None, :] // HEADDIM).astype(BF16)

    def by_rows(width):
        return pl.BlockSpec((CHUNK, width), lambda g, c, idx: (c, 0))

    def by_both(width):
        return pl.BlockSpec((CHUNK, width), lambda g, c, idx: (c, g))

    def by_group(height, width):
        return pl.BlockSpec((height, width), lambda g, c, idx: (0, g))

    def init(k):
        return pl.BlockSpec((1, WIDTH, STATE), lambda g, c, idx: (idx[k], g, 0))

    per_group = pl.BlockSpec((1, CHUNK, LANES), lambda g, c, idx: (g, c, 0))
    grid_spec = pltpu.PrefetchScalarGridSpec(
        num_scalar_prefetch=1,
        grid=(groups, chunks),
        in_specs=[
            by_both(WIDTH),
            by_both(2 * STATE),
            per_group,
            per_group,
            by_rows(LANES),
            pl.BlockSpec((8, CHUNK), lambda g, c, idx: (0, c)),
            by_rows(LANES),
            by_rows(32),
            by_group(32, WIDTH),
            by_group(32, 2 * STATE),
            by_group(5, WIDTH),
            by_group(5, 2 * STATE),
            by_group(1, WIDTH),
            pl.BlockSpec((2 * LANES, WIDTH), lambda g, c, idx: (0, 0)),
            init(0),
            init(1),
            init(2),
            init(3),
        ],
        out_specs=[
            by_both(WIDTH),
            pl.BlockSpec((SLOTS, WIDTH, STATE), lambda g, c, idx: (0, g, 0)),
        ],
        scratch_shapes=[
            pltpu.VMEM((SLOTS * STATE, WIDTH), F32),
            pltpu.VMEM((CHUNK + 8, WIDTH), F32),
            pltpu.VMEM((CHUNK + 8, 2 * STATE), F32),
            pltpu.VMEM((CHUNK, WIDTH), BF16),
            pltpu.VMEM((CHUNK, WIDTH), F32),
        ],
    )
    return pl.pallas_call(
        scan_kernel,
        grid_spec=grid_spec,
        out_shape=[
            jax.ShapeDtypeStruct((rows, groups * WIDTH), F32),
            jax.ShapeDtypeStruct((SLOTS, groups * WIDTH, STATE), F32),
        ],
        compiler_params=pltpu.CompilerParams(
            dimension_semantics=("arbitrary", "arbitrary"), vmem_limit_bytes=48 << 20
        ),
        cost_estimate=pl.CostEstimate(
            flops=40_000_000_000, bytes_accessed=30 << 20, transcendentals=20_000_000
        ),
        name="scan",
    )(idx, x_rows, bc_rows, dt, logs, segc, segr, pos, pick, fix_x, fix_bc, par_x, par_bc, skip, spread, states, states, states, states)


def run_gate(y, z_rows, gain):
    rows, width = y.shape
    block = pl.BlockSpec((CHUNK, WIDTH), lambda g, c: (c, g))
    return pl.pallas_call(
        gate_kernel,
        grid=(width // WIDTH, rows // CHUNK),
        in_specs=[block, block, pl.BlockSpec((1, WIDTH), lambda g, c: (0, g))],
        out_specs=block,
        out_shape=jax.ShapeDtypeStruct((rows, width), BF16),
        compiler_params=pltpu.CompilerParams(
            dimension_semantics=("arbitrary", "arbitrary"), vmem_limit_bytes=32 << 20
        ),
        cost_estimate=pl.CostEstimate(
            flops=40_000_000, bytes_accessed=16 << 20, transcendentals=2_000_000
        ),
        name="gate",
    )(y, z_rows, gain[None, :])


def shifted(value, axis, steps):
    count = lax.axis_size(axis)
    pairs = [(source, (source + steps) % count) for source in range(count)]
    return lax.ppermute(value, axis, pairs)


def exchanged(value):
    return lax.all_to_all(value, "tensor", split_axis=1, concat_axis=0, tiled=True)


def plan_rows(owner_idx, lengths, prefill_owner, row_start):
    match = prefill_owner == owner_idx
    earlier = match[None, :] & (row_start[None, :] < row_start[:, None])
    rank = jnp.sum(earlier.astype(jnp.int32), axis=1)
    chosen = match[None, :] & (rank[None, :] == jnp.arange(SLOTS, dtype=jnp.int32)[:, None])

    def pick(values):
        return jnp.sum(jnp.where(chosen, values[None, :], 0), axis=1)

    ids = jnp.arange(prefill_owner.shape[0], dtype=jnp.int32)
    return pick(ids), pick(row_start), pick(lengths)


def fixes(param, state):
    rows = []
    for at in range(3):
        rows.append(sum(param[3 - lag][None, :] * state[:, 3 - lag + at] for lag in range(at + 1, 4)))
    fix = jnp.stack(rows, axis=1).reshape(SLOTS * 3, -1)
    fix = jnp.pad(fix, ((0, 4), (0, 0)))
    high = fix.astype(BF16)
    low = (fix - lax.optimization_barrier(high).astype(F32)).astype(BF16)
    return jnp.concatenate([high, low], axis=0)


def shards(
    x_in,
    z_in,
    bc_in,
    dt_in,
    conv_x_param,
    conv_bc_param,
    decay_rate,
    dt_bias,
    skip_gain,
    norm_gain,
    ssm_state,
    conv_x_state,
    conv_bc_state,
    lengths,
    prefill_owner,
    row_start,
):
    dp_count = lax.axis_size("dp")
    my_index = lax.axis_index("dp")
    left_index = (my_index + dp_count - 1) % dp_count
    right_index = (my_index + 1) % dp_count
    slot_iota = jnp.arange(SLOTS, dtype=jnp.int32)
    my_dest = lax.dynamic_slice_in_dim(prefill_owner, my_index * SLOTS, SLOTS)
    right_slot = jnp.sum(jnp.where(my_dest == right_index, slot_iota, 0))
    left_slot = jnp.sum(jnp.where(my_dest == left_index, slot_iota, 0))
    conv_ids, starts, seg_lengths = plan_rows(my_index, lengths, prefill_owner, row_start)
    homes = conv_ids // SLOTS

    heads = ssm_state.shape[1]
    channels = heads * HEADDIM
    groups = heads // PER_GROUP
    own = ssm_state.reshape(SLOTS, channels, STATE)
    own_conv = jnp.concatenate([conv_x_state, conv_bc_state], axis=2)

    def taken(array, index):
        return lax.dynamic_slice_in_dim(array, index, 1, 0)

    from_left = shifted(taken(own, right_slot), "dp", 1)
    from_right = shifted(taken(own, left_slot), "dp", -1)
    conv_left = shifted(taken(own_conv, right_slot), "dp", 1)
    conv_right = shifted(taken(own_conv, left_slot), "dp", -1)

    dt_rows = exchanged(dt_in)
    bc_rows = exchanged(bc_in)
    x_rows = exchanged(x_in)
    z_tied, x_rows, bc_rows, dt_rows = lax.optimization_barrier((z_in, x_rows, bc_rows, dt_rows))
    z_rows = exchanged(z_tied)
    row_count = x_rows.shape[0]

    states = jnp.concatenate([own, from_left, from_right], axis=0)
    where_from = jnp.where(
        homes == my_index, conv_ids % SLOTS, jnp.where(homes == left_index, SLOTS, SLOTS + 1)
    ).astype(jnp.int32)
    convs = jnp.concatenate([own_conv, conv_left, conv_right], axis=0)
    initial_conv = jnp.concatenate([taken(convs, where_from[k]) for k in range(SLOTS)], axis=0)

    row_idx = jnp.arange(row_count, dtype=jnp.int32)
    segment = jnp.sum((row_idx[:, None] >= starts[None, :]).astype(jnp.int32), axis=1) - 1
    begin = jnp.max(jnp.where(row_idx[:, None] >= starts[None, :], starts[None, :], 0), axis=1)
    position = row_idx - begin
    segc = jnp.broadcast_to(segment.astype(F32)[:, None], (row_count, LANES))
    segr = jnp.broadcast_to(segment.astype(F32)[None, :], (8, row_count))
    pos = jnp.broadcast_to(position[:, None], (row_count, LANES))
    code = jnp.where(position < 3, segment * 3 + position, 15)
    pick = (code[:, None] == jnp.arange(32, dtype=jnp.int32)[None, :] % 16).astype(BF16)

    def grouped(value, fill):
        value = jnp.transpose(value.reshape(row_count, groups, PER_GROUP), (1, 0, 2))
        return jnp.pad(value, ((0, 0), (0, 0), (0, LANES - PER_GROUP)), constant_values=fill)

    dt = jax.nn.softplus(dt_rows.astype(F32) + dt_bias[None, :])
    logs = dt * (decay_rate * (-LOG2E))[None, :]
    y, finals = run_scan(
        where_from,
        x_rows,
        bc_rows,
        grouped(dt, 1.0),
        grouped(logs, 0.0),
        segc,
        segr,
        pos,
        pick,
        fixes(conv_x_param, initial_conv[:, :, :channels]),
        fixes(conv_bc_param, initial_conv[:, :, channels:]),
        conv_x_param,
        conv_bc_param,
        jnp.repeat(skip_gain, HEADDIM)[None, :],
        states,
    )
    y_out = run_gate(y, z_rows, norm_gain)

    lasts = []
    for k in range(SLOTS):
        at = starts[k] + seg_lengths[k] - 3
        lasts.append(
            jnp.concatenate(
                [
                    lax.dynamic_slice_in_dim(x_rows, at, 3, 0),
                    lax.dynamic_slice_in_dim(bc_rows, at, 3, 0),
                ],
                axis=1,
            )
        )
    lasts = jnp.stack(lasts, axis=0)
    left_at = jnp.sum(jnp.where(homes == left_index, slot_iota, 0))
    right_at = jnp.sum(jnp.where(homes == right_index, slot_iota, 0))
    back_right = shifted(taken(finals, left_at).astype(BF16), "dp", -1)
    back_left = shifted(taken(finals, right_at).astype(BF16), "dp", 1)
    last_right = shifted(taken(lasts, left_at), "dp", -1)
    last_left = shifted(taken(lasts, right_at), "dp", 1)

    def gathered(mine, right, left):
        pieces = []
        for s in range(SLOTS):
            at = jnp.sum(jnp.where(conv_ids == my_index * SLOTS + s, slot_iota, 0))
            there = jnp.where(my_dest[s] == right_index, right, left).astype(F32)
            here = taken(mine, at).astype(F32)
            pieces.append(jnp.where(my_dest[s] == my_index, here, there))
        return jnp.concatenate(pieces, axis=0)

    new_ssm = gathered(finals, back_right, back_left).reshape(ssm_state.shape)
    new_conv = gathered(lasts, last_right, last_left)
    return (y_out, new_ssm, new_conv[:, :, :channels], new_conv[:, :, channels:])


def solution(mesh):
    in_specs = (
        P(("dp", "tensor"), None),
        P(("dp", "tensor"), None),
        P(("dp", "tensor"), None),
        P(("dp", "tensor"), None),
        P(None, "tensor"),
        P(None, "tensor"),
        P("tensor"),
        P("tensor"),
        P("tensor"),
        P("tensor"),
        P("dp", "tensor", None, None),
        P("dp", None, "tensor"),
        P("dp", None, "tensor"),
        P(),
        P(),
        P(),
    )
    out_specs = (
        P("dp", "tensor"),
        P("dp", "tensor", None, None),
        P("dp", None, "tensor"),
        P("dp", None, "tensor"),
    )
    return jax.shard_map(shards, mesh=mesh, in_specs=in_specs, out_specs=out_specs, check_vma=False)
```

time: 864 us -> 257 us (0.30); the launches traced: 853 us -> 256 us
  matrix products: 315 us -> 0 us
  local copies, waits for them, and re-layouts: 226 us -> 27.5 us
  other arithmetic: 103 us -> 14.3 us
  loops' own time: 80.9 us -> 0 us
  Pallas kernels: 0 us -> 45 us
  between operations: 3.13 us -> 34 us
  waiting for transfers between devices: 89.4 us -> 109 us
    dot_general x154 -> x0, matrix products: 306 us -> none  [the longest x32 159 us: head_scan(): output = jnp.dot(scores, x_head, preferred_element_type=jnp.float32)]
    dynamic_slice x160 -> x6, local copies, waits for them, and re-layouts: 86.3 us -> 4.21 us  [the longest x4 3.2 us: taken(): return lax.dynamic_slice_in_dim(array, index, 1, 0)]
    another operation x2 -> x0, loops' own time: 80.9 us -> none  [group_block(): lax.map(one_head, jnp.arange(HEADS // GROUPS, dtype=jnp.int32))]
    gather x100 -> x0, local copies, waits for them, and re-layouts: 62.9 us -> none  [the longest x64 40.2 us: head_scan(): before = running[starts] - log_decay[starts]]
    all_to_all x4, waiting for transfers between devices: 44.4 us -> 96.7 us  [exchanged(): lax.all_to_all(value, 'tensor', split_axis=1, concat_axis=0, tiled=True)]
    mul x96 -> x2, other arithmetic: 51.5 us -> 0.66 us  [shards(): logs = dt * (decay_rate * -LOG2E)[None, :]]
    pallas_call x0 -> x2, Pallas kernels: none -> 45 us  [the longest x1 37.1 us: run_scan(): pl.pallas_call(scan_kernel, grid_spec=grid_spec, out_shape=[jax.ShapeDtyp...]
    ppermute x12 -> x8, waiting for transfers between devices: 45 us -> 11.8 us  [shifted(): return lax.ppermute(value, axis, pairs)]
  transfers between devices with their start and end apart: 16 -> 12, of which waited for: 5 -> 6; matrix products, arithmetic and copies ran while one was open for 74% -> 12% of each run, Pallas kernels for 0% -> 15%
where the time goes in v1:
time: 257 us; the launch traced here: 256 us
  waiting for transfers between devices  109 us (42%)
  Pallas kernels  45 us (18%)
  between operations  34 us (13%)
  local copies, waits for them, and re-layouts  27.5 us (11%)
  starting transfers between devices  26.3 us (10%)
  other arithmetic  14.3 us (6%)
    all_to_all x4, waiting for transfers between devices, exchanged(): lax.all_to_all(value, 'tensor', split_axis=1, concat_axis=0, tiled=True)  96.7 us
    pallas_call x1, Pallas kernels, run_scan(): pl.pallas_call(scan_kernel, grid_spec=grid_spec, out_shape=[jax.ShapeDtyp...  37.1 us
    all_to_all x4, starting transfers between devices, exchanged(): lax.all_to_all(value, 'tensor', split_axis=1, concat_axis=0, tiled=True)  19.7 us
    ppermute x8, waiting for transfers between devices, shifted(): return lax.ppermute(value, axis, pairs)  11.8 us
    all_to_all x4, local copies, waits for them, and re-layouts, exchanged(): lax.all_to_all(value, 'tensor', split_axis=1, concat_axis=0, tiled=True)  9.41 us
    pallas_call x1, Pallas kernels, run_gate(): pl.pallas_call(gate_kernel, grid=(width // WIDTH, rows // CHUNK), in_spec...  7.89 us
    ppermute x8, starting transfers between devices, shifted(): return lax.ppermute(value, axis, pairs)  6.58 us
    unnamed x32, local copies, waits for them, and re-layouts  6.4 us
  transfers between devices with their start and end apart: 12, of which 6 were waited for; matrix products, arithmetic and copies ran while one was open for 12% of the time, Pallas kernels for 15%

profile of v1, /device:TPU:0, one launch (start us, length us, event | category | flops | bytes accessed | tf_op | source)
XLA Modules:
  0.0 255.7 jit_solution(3042307068978123624)
XLA Ops:
  0.7 1.6 copy.51
  2.3 6.3 %all-to-all-start.2 = ((bf16[256,4,32]{0,2,1:T(8,128)(2,1)}), bf16[256,4,32]{0,2,1:T(8,128)(2,1)S(1)}, u32[]{:S(2)}, u32[]{:S(2)}) async-start(bf16[256,4,32]{0,2,1:T(8,128)(2,1)} %bitcast.4), calls=%async_computation.2 | async-start | bytes 131072 | tf_op jit(solution)/shard_map/all_to_all | solution.py:274
  9.3 2.3 copy.70
  11.6 2.8 %all-to-all-done.2 = bf16[256,4,32]{0,2,1:T(8,128)(2,1)S(1)} async-done(((bf16[256,4,32]{0,2,1:T(8,128)(2,1)}), bf16[256,4,32]{0,2,1:T(8,128)(2,1)S(1)}, u32[]{:S(2)}, u32[]{:S(2)}) %all-to-all-start.2) | async-done | bytes 65568 | tf_op jit(solution)/shard_map/all_to_all | solution.py:274
  14.4 3.5 %all-to-all-start.1 = ((bf16[256,4,512]{2,0,1:T(8,128)(2,1)}), bf16[256,4,512]{2,0,1:T(8,128)(2,1)S(1)}, u32[]{:S(2)}, u32[]{:S(2)}) async-start(bf16[256,4,512]{2,0,1:T(8,128)(2,1)} %bitcast.61), calls=%async_computation.1 | async-start | bytes 2097152 | tf_op jit(solution)/shard_map/all_to_all | solution.py:274
  23.7 3.0 %constant_dynamic-slice_fusion.11 = (f32[1,2048,128]{2,1,0:T(8,128)S(1)}, f32[1,2048,128]{2,1,0:T(8,128)}) fusion(f32[4,2048,128]{2,1,0:T(8,128)} %bitcast.67, s32[]{:T(128)S(6)} %select_n.298, s32[]{:T(128)S(6)} %select_n.300), kind=kLoop, calls=%fused_computation.63 | loop fusion | bytes 4194312 | tf_op jit(solution)/shard_map/dynamic_slice | solution.py:337
  26.7 2.3 collective-permute-start.3
  29.0 2.3 copy.69
  31.3 11.1 %all-to-all-done.1 = bf16[256,4,512]{2,0,1:T(8,128)(2,1)S(1)} async-done(((bf16[256,4,512]{2,0,1:T(8,128)(2,1)}), bf16[256,4,512]{2,0,1:T(8,128)(2,1)S(1)}, u32[]{:S(2)}, u32[]{:S(2)}) %all-to-all-start.1) | async-done | bytes 1048608 | tf_op jit(solution)/shard_map/all_to_all | solution.py:274
  42.4 5.0 %all-to-all-start = ((bf16[256,4,2048]{2,0,1:T(8,128)(2,1)}), bf16[256,4,2048]{2,0,1:T(8,128)(2,1)}, u32[]{:S(2)}, u32[]{:S(2)}) async-start(bf16[256,4,2048]{2,0,1:T(8,128)(2,1)} %bitcast.65), calls=%async_computation | async-start | bytes 8388608 | tf_op jit(solution)/shard_map/all_to_all | solution.py:274
  80.5 5.9 %pad_maximum_fusion.init0.init1.init2.init3 = f32[6,2048,128]{2,1,0:T(8,128)} fusion(f32[1,2048,128]{2,1,0:T(8,128)} %collective-permute-done.3, f32[1,2048,128]{2,1,0:T(8,128)} %collective-permute-done.2, f32[4,2048,128]{2,1,0:T(8,128)} %bitcast.68), kind=kLoop, calls=%fused_computation | loop fusion | flops 3145728 | bytes 12582912 | tf_op jit(solution)/shard_map/concatenate | solution.py:351
  86.5 53.8 %all-to-all-done = bf16[256,4,2048]{2,0,1:T(8,128)(2,1)} async-done(((bf16[256,4,2048]{2,0,1:T(8,128)(2,1)}), bf16[256,4,2048]{2,0,1:T(8,128)(2,1)}, u32[]{:S(2)}, u32[]{:S(2)}) %all-to-all-start) | async-done | bytes 4194336 | tf_op jit(solution)/shard_map/all_to_all | solution.py:274
  142.0 4.8 %copy.68 = bf16[32,4,8,2048]{3,2,0,1:T(8,128)(2,1)} copy(bf16[32,4,8,2048]{3,2,1,0:T(8,128)(2,1)} %bitcast.72) | data formatting | bytes 8388608 | tf_op jit(solution)/shard_map/all_to_all | solution.py:274
  146.8 4.9 %all-to-all-start.3 = ((bf16[256,4,2048]{2,0,1:T(8,128)(2,1)}), bf16[256,4,2048]{2,0,1:T(8,128)(2,1)}, u32[]{:S(2)}, u32[]{:S(2)}) async-start(bf16[256,4,2048]{2,0,1:T(8,128)(2,1)} %bitcast.66), calls=%async_computation.3 | async-start | bytes 8388608 | tf_op jit(solution)/shard_map/all_to_all | solution.py:274
  155.8 37.1 %scan.1 = (f32[1024,2048]{1,0:T(8,128)}, f32[4,2048,128]{2,1,0:T(8,128)}) custom-call(s32[4]{0:T(128)S(1)} %compare_select_fusion.8.idx_ref, bf16[1024,2048]{1,0:T(8,128)(2,1)} %bitcast.1.x_ref, bf16[1024,512]{1,0:T(8,128)(2,1)S(1)} %bitcast.63, f32[2,1024,128]{2,1,0:T(8,128)S(1)} %pad.15.dt_ref, f32[2,1024,128]{2,1,0:T(8,128)S(1)} %pad.16.log_ref, ...), custom_call_target="tpu_custom_call" | custom-call | flops 40000000000 | bytes 31457280 | tf_op jit(solution)/shard_map/scan/pallas_call | solution.py:231
  192.9 1.7 dynamic-slice_convert_fusion
  194.5 2.7 %collective-permute-start.4 = (bf16[1,2048,128]{2,1,0:T(8,128)(2,1)S(1)}, bf16[1,2048,128]{2,1,0:T(8,128)(2,1)S(1)}, u32[]{:S(2)}, u32[]{:S(2)}) collective-permute-start(bf16[1,2048,128]{2,1,0:T(8,128)(2,1)S(1)} %get-tuple-element.58), channel_id=1, source_target_pairs={{0,28},{4,0},{8,4},{12,8},{16,12},{20,16},{24,20},{28,24},{1,29},{... | collective-permute-start | bytes 1572872 | tf_op jit(solution)/shard_map/ppermute | solution.py:270
  198.7 9.8 %collective-permute-done.4 = bf16[1,2048,128]{2,1,0:T(8,128)(2,1)S(1)} collective-permute-done((bf16[1,2048,128]{2,1,0:T(8,128)(2,1)S(1)}, bf16[1,2048,128]{2,1,0:T(8,128)(2,1)S(1)}, u32[]{:S(2)}, u32[]{:S(2)}) %collective-permute-start.4) | collective-permute-done | bytes 524320 | tf_op jit(solution)/shard_map/ppermute | solution.py:270
  208.5 2.0 collective-permute-done.5
  210.5 2.6 %convert_select_fusion.3 = (f32[1,2048,128]{2,1,0:T(8,128)S(1)}, f32[1,2048,128]{2,1,0:T(8,128)S(1)}, f32[1,2048,128]{2,1,0:T(8,128)S(1)}, f32[1,2048,128]{2,1,0:T(8,128)S(1)}) fusion(f32[4,2048,128]{2,1,0:T(8,128)} %get-tuple-element.15, s32[]{:T(128)S(6)} %select_n.309, bf16[1,2048,128]{2,1,0:T(8,128)(2,1)S(1)} %collective-permute-done.4, ...), kind=kLoop, calls=%fused_computation.8 | loop fusion | flops 3145728 | bytes 9437208 | tf_op jit(solution)/shard_map/jit(_where)/select_n | solution.py:419
  213.1 2.3 pad_maximum_fusion.1
  215.4 29.0 %all-to-all-done.3 = bf16[256,4,2048]{2,0,1:T(8,128)(2,1)} async-done(((bf16[256,4,2048]{2,0,1:T(8,128)(2,1)}), bf16[256,4,2048]{2,0,1:T(8,128)(2,1)}, u32[]{:S(2)}, u32[]{:S(2)}) %all-to-all-start.3) | async-done | bytes 4194336 | tf_op jit(solution)/shard_map/all_to_all | solution.py:274
  244.4 3.4 %copy-done = f32[1024,2048]{1,0:T(8,128)S(1)} copy-done((f32[1024,2048]{1,0:T(8,128)S(1)}, f32[1024,2048]{1,0:T(8,128)}, u32[]{:S(2)}) %copy-start) | copy-done | bytes 8388632
  247.8 7.9 %gate.1 = bf16[1024,2048]{1,0:T(8,128)(2,1)} custom-call(f32[1024,2048]{1,0:T(8,128)S(1)} %copy-done, bf16[1024,2048]{1,0:T(8,128)(2,1)} %bitcast.22.z_ref, f32[1,2048]{1,0:T(1,128)S(1)} %bitcast.64), custom_call_target="tpu_custom_call" | custom-call | flops 40000000 | bytes 16777216 | tf_op jit(solution)/shard_map/gate/pallas_call | solution.py:251
  (103 shorter events, 13.6 us)
Async XLA Ops:
  0.6 17.6 %copy-start.11 = (s32[32]{0:T(128)S(1)}, s32[32]{0:T(128)}, u32[]{:S(2)}) copy-start(s32[32]{0:T(128)} %param.30) | copy-start | bytes 388
  0.6 17.3 %copy-start.7 = (s32[32]{0:T(128)S(1)}, s32[32]{0:T(128)}, u32[]{:S(2)}) copy-start(s32[32]{0:T(128)} %param.31) | copy-start | bytes 388
  0.7 17.5 %copy-start.10 = (s32[32]{0:T(128)S(1)}, s32[32]{0:T(128)}, u32[]{:S(2)}) copy-start(s32[32]{0:T(128)} %param.29) | copy-start | bytes 388
  0.7 22.3 %copy-start.5 = (f32[4,3,2048]{2,0,1:T(4,128)S(1)}, f32[4,3,2048]{2,0,1:T(4,128)}, u32[]{:S(2)}) copy-start(f32[4,3,2048]{2,0,1:T(4,128)} %param.27) | copy-start | bytes 294916
  0.7 22.4 %copy-start.6 = (f32[4,3,512]{2,0,1:T(4,128)S(1)}, f32[4,3,512]{2,0,1:T(4,128)}, u32[]{:S(2)}) copy-start(f32[4,3,512]{2,0,1:T(4,128)} %param.28) | copy-start | bytes 73732
  2.3 12.1 %all-to-all-start.2 = ((bf16[256,4,32]{0,2,1:T(8,128)(2,1)}), bf16[256,4,32]{0,2,1:T(8,128)(2,1)S(1)}, u32[]{:S(2)}, u32[]{:S(2)}) async-start(bf16[256,4,32]{0,2,1:T(8,128)(2,1)} %bitcast.4), calls=%async_computation.2 | async-start | bytes 131072 | tf_op jit(solution)/shard_map/all_to_all | solution.py:274
  14.4 28.1 %all-to-all-start.1 = ((bf16[256,4,512]{2,0,1:T(8,128)(2,1)}), bf16[256,4,512]{2,0,1:T(8,128)(2,1)S(1)}, u32[]{:S(2)}, u32[]{:S(2)}) async-start(bf16[256,4,512]{2,0,1:T(8,128)(2,1)} %bitcast.61), calls=%async_computation.1 | async-start | bytes 2097152 | tf_op jit(solution)/shard_map/all_to_all | solution.py:274
  23.1 56.5 %collective-permute-start.1 = (f32[1,3,2560]{2,0,1:T(1,128)S(1)}, f32[1,3,2560]{2,0,1:T(1,128)S(1)}, u32[]{:S(2)}, u32[]{:S(2)}) collective-permute-start(f32[1,3,2560]{2,0,1:T(1,128)S(1)} %get-tuple-element.77), channel_id=1, source_target_pairs={{0,28},{4,0},{8,4},{12,8},{16,12},{20,16},{24,20},{28,24},{1,29},{... | collective-permute-start | bytes 92168 | tf_op jit(solution)/shard_map/ppermute | solution.py:270
  23.6 56.0 %collective-permute-start = (f32[1,3,2560]{2,0,1:T(1,128)S(1)}, f32[1,3,2560]{2,0,1:T(1,128)S(1)}, u32[]{:S(2)}, u32[]{:S(2)}) collective-permute-start(f32[1,3,2560]{2,0,1:T(1,128)S(1)} %get-tuple-element.76), channel_id=1, source_target_pairs={{0,4},{4,8},{8,12},{12,16},{16,20},{20,24},{24,28},{28,0},{1,5},{5... | collective-permute-start | bytes 92168 | tf_op jit(solution)/shard_map/ppermute | solution.py:270
  26.7 53.8 %collective-permute-start.3 = (f32[1,2048,128]{2,1,0:T(8,128)}, f32[1,2048,128]{2,1,0:T(8,128)}, u32[]{:S(2)}, u32[]{:S(2)}) collective-permute-start(f32[1,2048,128]{2,1,0:T(8,128)} %get-tuple-element.60), channel_id=1, source_target_pairs={{0,28},{4,0},{8,4},{12,8},{16,12},{20,16},{24,20},{28,24},{1,29},{... | collective-permute-start | bytes 3145736 | tf_op jit(solution)/shard_map/ppermute | solution.py:270
  28.9 51.6 %collective-permute-start.2 = (f32[1,2048,128]{2,1,0:T(8,128)S(1)}, f32[1,2048,128]{2,1,0:T(8,128)}, u32[]{:S(2)}, u32[]{:S(2)}) collective-permute-start(f32[1,2048,128]{2,1,0:T(8,128)S(1)} %get-tuple-element.59), channel_id=1, source_target_pairs={{0,4},{4,8},{8,12},{12,16},{16,20},{20,24},{24,28},{28,0},{1,5},{5... | collective-permute-start | bytes 3145736 | tf_op jit(solution)/shard_map/ppermute | solution.py:270
  42.4 6.5 %copy-start.13 = (f32[32]{0:T(128)S(1)}, f32[32]{0:T(128)}, u32[]{:S(2)}) copy-start(f32[32]{0:T(128)} %param.22) | copy-start | bytes 388
  42.4 7.0 %copy-start.3 = (f32[5,512]{1,0:T(8,128)S(1)}, f32[5,512]{1,0:T(8,128)}, u32[]{:S(2)}) copy-start(f32[5,512]{1,0:T(8,128)} %par_bc_ref.1) | copy-start | bytes 30724
  42.4 7.4 %copy-start.1 = (f32[5,2048]{1,0:T(8,128)S(1)}, f32[5,2048]{1,0:T(8,128)}, u32[]{:S(2)}) copy-start(f32[5,2048]{1,0:T(8,128)} %par_x_ref.1) | copy-start | bytes 122884
  42.4 30.7 %copy-start.12 = (f32[32]{0:T(128)S(1)}, f32[32]{0:T(128)}, u32[]{:S(2)}) copy-start(f32[32]{0:T(128)} %param.24) | copy-start | bytes 388
  42.4 97.8 %all-to-all-start = ((bf16[256,4,2048]{2,0,1:T(8,128)(2,1)}), bf16[256,4,2048]{2,0,1:T(8,128)(2,1)}, u32[]{:S(2)}, u32[]{:S(2)}) async-start(bf16[256,4,2048]{2,0,1:T(8,128)(2,1)} %bitcast.65), calls=%async_computation | async-start | bytes 8388608 | tf_op jit(solution)/shard_map/all_to_all | solution.py:274
  80.5 59.8 %copy-start.8 = (f32[32]{0:T(128)S(1)}, f32[32]{0:T(128)}, u32[]{:S(2)}) copy-start(f32[32]{0:T(128)} %param.23) | copy-start | bytes 388
  80.5 59.7 %copy-start.9 = (f32[32]{0:T(128)S(1)}, f32[32]{0:T(128)}, u32[]{:S(2)}) copy-start(f32[32]{0:T(128)} %broadcast_multiply_fusion.2) | copy-start | bytes 388
  146.8 97.5 %all-to-all-start.3 = ((bf16[256,4,2048]{2,0,1:T(8,128)(2,1)}), bf16[256,4,2048]{2,0,1:T(8,128)(2,1)}, u32[]{:S(2)}, u32[]{:S(2)}) async-start(bf16[256,4,2048]{2,0,1:T(8,128)(2,1)} %bitcast.66), calls=%async_computation.3 | async-start | bytes 8388608 | tf_op jit(solution)/shard_map/all_to_all | solution.py:274
  152.9 44.3 %collective-permute-start.6 = (bf16[1,3,2560]{2,1,0:T(4,128)(2,1)S(1)}, bf16[1,3,2560]{2,1,0:T(4,128)(2,1)S(1)}, u32[]{:S(2)}, u32[]{:S(2)}) collective-permute-start(bf16[1,3,2560]{2,1,0:T(4,128)(2,1)S(1)} %get-tuple-element.79), channel_id=1, source_target_pairs={{0,28},{4,0},{8,4},{12,8},{16,12},{20,16},{24,20},{28,24},{1,29},{... | collective-permute-start | bytes 46088 | tf_op jit(solution)/shard_map/ppermute | solution.py:270
  154.0 43.3 %collective-permute-start.7 = (bf16[1,3,2560]{2,1,0:T(4,128)(2,1)S(1)}, bf16[1,3,2560]{2,1,0:T(4,128)(2,1)S(1)}, u32[]{:S(2)}, u32[]{:S(2)}) collective-permute-start(bf16[1,3,2560]{2,1,0:T(4,128)(2,1)S(1)} %get-tuple-element.78), channel_id=1, source_target_pairs={{0,4},{4,8},{8,12},{12,16},{16,20},{20,24},{24,28},{28,0},{1,5},{5... | collective-permute-start | bytes 46088 | tf_op jit(solution)/shard_map/ppermute | solution.py:270
  194.5 14.0 %collective-permute-start.4 = (bf16[1,2048,128]{2,1,0:T(8,128)(2,1)S(1)}, bf16[1,2048,128]{2,1,0:T(8,128)(2,1)S(1)}, u32[]{:S(2)}, u32[]{:S(2)}) collective-permute-start(bf16[1,2048,128]{2,1,0:T(8,128)(2,1)S(1)} %get-tuple-element.58), channel_id=1, source_target_pairs={{0,28},{4,0},{8,4},{12,8},{16,12},{20,16},{24,20},{28,24},{1,29},{... | collective-permute-start | bytes 1572872 | tf_op jit(solution)/shard_map/ppermute | solution.py:270
  197.2 13.3 %collective-permute-start.5 = (bf16[1,2048,128]{2,1,0:T(8,128)(2,1)S(1)}, bf16[1,2048,128]{2,1,0:T(8,128)(2,1)S(1)}, u32[]{:S(2)}, u32[]{:S(2)}) collective-permute-start(bf16[1,2048,128]{2,1,0:T(8,128)(2,1)S(1)} %get-tuple-element.57), channel_id=1, source_target_pairs={{0,4},{4,8},{8,12},{12,16},{16,20},{20,24},{24,28},{28,0},{1,5},{5... | collective-permute-start | bytes 1572872 | tf_op jit(solution)/shard_map/ppermute | solution.py:270
  213.1 31.3 %copy-start.2 = (f32[2048]{0:T(1024)S(1)}, f32[2048]{0:T(1024)}, u32[]{:S(2)}) copy-start(f32[2048]{0:T(1024)} %param.25) | copy-start | bytes 24580
  (2 other events, 9.3 us)

commit v2 on v1

--- a/solution.py
+++ b/solution.py
@@ -173,9 +173,9 @@
     out_ref[...] = (gated * lax.rsqrt(square + EPSILON) * gain_ref[...]).astype(BF16)
 
 
-def run_scan(idx, x_rows, bc_rows, dt, logs, segc, segr, pos, pick, fix_x, fix_bc, par_x, par_bc, skip, states):
-    rows = x_rows.shape[0]
-    groups = x_rows.shape[1] // WIDTH
+def run_scan(idx, mixed, groups, dt, logs, segc, segr, pos, pick, fix_x, fix_bc, par_x, par_bc, skip, states):
+    rows = mixed.shape[0]
+    bc_first = groups * WIDTH // (2 * STATE)
     chunks = rows // CHUNK
     heads = jnp.arange(2 * LANES, dtype=jnp.int32)[:, None] % LANES
     spread = (heads == jnp.arange(WIDTH, dtype=jnp.int32)[None, :] // HEADDIM).astype(BF16)
@@ -198,7 +198,7 @@
         grid=(groups, chunks),
         in_specs=[
             by_both(WIDTH),
-            by_both(2 * STATE),
+            pl.BlockSpec((CHUNK, 2 * STATE), lambda g, c, idx: (c, bc_first + g)),
             per_group,
             per_group,
             by_rows(LANES),
@@ -242,7 +242,7 @@
             flops=40_000_000_000, bytes_accessed=30 << 20, transcendentals=20_000_000
         ),
         name="scan",
-    )(idx, x_rows, bc_rows, dt, logs, segc, segr, pos, pick, fix_x, fix_bc, par_x, par_bc, skip, spread, states, states, states, states)
+    )(idx, mixed, mixed, dt, logs, segc, segr, pos, pick, fix_x, fix_bc, par_x, par_bc, skip, spread, states, states, states, states)
 
 
 def run_gate(y, z_rows, gain):
@@ -255,7 +255,7 @@
         out_specs=block,
         out_shape=jax.ShapeDtypeStruct((rows, width), BF16),
         compiler_params=pltpu.CompilerParams(
-            dimension_semantics=("arbitrary", "arbitrary"), vmem_limit_bytes=32 << 20
+            dimension_semantics=("arbitrary", "arbitrary"), vmem_limit_bytes=56 << 20
         ),
         cost_estimate=pl.CostEstimate(
             flops=40_000_000, bytes_accessed=16 << 20, transcendentals=2_000_000
@@ -271,7 +271,8 @@
 
 
 def exchanged(value):
-    return lax.all_to_all(value, "tensor", split_axis=1, concat_axis=0, tiled=True)
+    got = lax.all_to_all(value, "tensor", split_axis=0, concat_axis=0, tiled=True)
+    return got.reshape(-1, value.shape[2])
 
 
 def plan_rows(owner_idx, lengths, prefill_owner, row_start):
@@ -341,12 +342,18 @@
     conv_left = shifted(taken(own_conv, right_slot), "dp", 1)
     conv_right = shifted(taken(own_conv, left_slot), "dp", -1)
 
-    dt_rows = exchanged(dt_in)
-    bc_rows = exchanged(bc_in)
-    x_rows = exchanged(x_in)
-    z_tied, x_rows, bc_rows, dt_rows = lax.optimization_barrier((z_in, x_rows, bc_rows, dt_rows))
+    tensor_count = lax.axis_size("tensor")
+    bc_width = groups * 2 * STATE
+
+    def by_target(value):
+        return jnp.transpose(value.reshape(value.shape[0], tensor_count, -1), (1, 0, 2))
+
+    dt_parts = jnp.pad(by_target(dt_in), ((0, 0), (0, 0), (0, -heads % LANES)))
+    mixed = exchanged(jnp.concatenate([by_target(x_in), by_target(bc_in), dt_parts], axis=2))
+    z_tied, mixed = lax.optimization_barrier((by_target(z_in), mixed))
     z_rows = exchanged(z_tied)
-    row_count = x_rows.shape[0]
+    row_count = mixed.shape[0]
+    dt_rows = mixed[:, channels + bc_width : channels + bc_width + heads]
 
     states = jnp.concatenate([own, from_left, from_right], axis=0)
     where_from = jnp.where(
@@ -373,8 +380,8 @@
     logs = dt * (decay_rate * (-LOG2E))[None, :]
     y, finals = run_scan(
         where_from,
-        x_rows,
-        bc_rows,
+        mixed,
+        groups,
         grouped(dt, 1.0),
         grouped(logs, 0.0),
         segc,
@@ -393,15 +400,7 @@
     lasts = []
     for k in range(SLOTS):
         at = starts[k] + seg_lengths[k] - 3
-        lasts.append(
-            jnp.concatenate(
-                [
-                    lax.dynamic_slice_in_dim(x_rows, at, 3, 0),
-                    lax.dynamic_slice_in_dim(bc_rows, at, 3, 0),
-                ],
-                axis=1,
-            )
-        )
+        lasts.append(lax.dynamic_slice(mixed, (at, 0), (3, channels + bc_width)))
     lasts = jnp.stack(lasts, axis=0)
     left_at = jnp.sum(jnp.where(homes == left_index, slot_iota, 0))
     right_at = jnp.sum(jnp.where(homes == right_index, slot_iota, 0))

time: 257 us -> 250 us (0.973)
  local copies, waits for them, and re-layouts: 27.5 us -> 20.5 us
  starting transfers between devices: 26.3 us -> 20.1 us
  other arithmetic: 14.3 us -> 19.3 us
    all_to_all x4 -> x0, local copies, waits for them, and re-layouts: 9.41 us -> none  [exchanged(): lax.all_to_all(value, 'tensor', split_axis=1, concat_axis=0, tiled=True)]
    reshape x0 -> x3, local copies, waits for them, and re-layouts: none -> 8.6 us  [by_target(): value.reshape(value.shape[0], tensor_count, -1)]
    all_to_all x4 -> x2, starting transfers between devices: 19.7 us -> 11.3 us  [exchanged(): lax.all_to_all(value, 'tensor', split_axis=0, concat_axis=0, tiled=True)]
    concatenate x0 -> x1, other arithmetic: none -> 5.16 us  [shards(): jnp.concatenate([by_target(x_in), by_target(bc_in), dt_parts], axis=2)]
    unnamed x32 -> x25, local copies, waits for them, and re-layouts: 6.4 us -> 2.49 us
    all_to_all x4 -> x2, waiting for transfers between devices: 96.7 us -> 95.6 us  [exchanged(): lax.all_to_all(value, 'tensor', split_axis=0, concat_axis=0, tiled=True)]
  transfers between devices with their start and end apart: 12 -> 10, of which waited for: 6 -> 4; matrix products, arithmetic and copies ran while one was open for 12% -> 11% of each run, Pallas kernels for 15% -> 15%
where the time goes in v2:
time: 250 us; the launch traced here: 249 us
  waiting for transfers between devices  108 us (43%)
  Pallas kernels  47.1 us (19%)
  between operations  34.1 us (14%)
  local copies, waits for them, and re-layouts  20.5 us (8%)
  starting transfers between devices  20.1 us (8%)
  other arithmetic  19.3 us (8%)
    all_to_all x2, waiting for transfers between devices, exchanged(): lax.all_to_all(value, 'tensor', split_axis=0, concat_axis=0, tiled=True)  95.6 us
    pallas_call x1, Pallas kernels, run_scan(): pl.pallas_call(scan_kernel, grid_spec=grid_spec, out_shape=[jax.ShapeDtyp...  37.4 us
    ppermute x8, waiting for transfers between devices, shifted(): return lax.ppermute(value, axis, pairs)  12 us
    all_to_all x2, starting transfers between devices, exchanged(): lax.all_to_all(value, 'tensor', split_axis=0, concat_axis=0, tiled=True)  11.3 us
    pallas_call x1, Pallas kernels, run_gate(): pl.pallas_call(gate_kernel, grid=(width // WIDTH, rows // CHUNK), in_spec...  9.62 us
    ppermute x8, starting transfers between devices, shifted(): return lax.ppermute(value, axis, pairs)  8.71 us
    reshape x3, local copies, waits for them, and re-layouts, by_target(): value.reshape(value.shape[0], tensor_count, -1)  8.6 us
    concatenate x1, other arithmetic, shards(): states = jnp.concatenate([own, from_left, from_right], axis=0)  5.62 us
  transfers between devices with their start and end apart: 10, of which 4 were waited for; matrix products, arithmetic and copies ran while one was open for 11% of the time, Pallas kernels for 15%

profile of v2, /device:TPU:0, one launch (start us, length us, event | category | flops | bytes accessed | tf_op | source)
XLA Modules:
  0.0 248.7 jit_solution(2275358080401409014)
XLA Ops:
  0.6 0.9 copy.55
  1.8 1.3 copy.76
  3.1 2.5 %copy.74 = bf16[32,4,8,2048]{3,2,0,1:T(8,128)(2,1)S(1)} copy(bf16[32,4,8,2048]{3,2,1,0:T(8,128)(2,1)} %bitcast.69) | data formatting | bytes 8388608 | tf_op jit(solution)/shard_map/reshape | solution.py:349
  5.6 5.2 %fusion.1 = bf16[4,256,2688]{2,1,0:T(8,128)(2,1)} fusion(bf16[4,256,32]{2,1,0:T(8,128)(2,1)S(1)} %copy.67, bf16[4,256,512]{2,1,0:T(8,128)(2,1)S(1)} %bitcast.72, bf16[4,256,2048]{2,1,0:T(8,128)(2,1)S(1)} %bitcast.64), kind=kLoop, calls=%fused_computation.3 | loop fusion | flops 22020096 | bytes 10813440 | tf_op jit(solution)/shard_map/concatenate | solution.py:352
  10.8 6.5 %all-to-all-start = ((bf16[4,256,2688]{2,1,0:T(8,128)(2,1)}), bf16[4,256,2688]{2,1,0:T(8,128)(2,1)}, u32[]{:S(2)}, u32[]{:S(2)}) async-start(bf16[4,256,2688]{2,1,0:T(8,128)(2,1)} %fusion.1), calls=%async_computation | async-start | bytes 11010048 | tf_op jit(solution)/shard_map/all_to_all | solution.py:274
  22.5 2.2 collective-permute-start.1
  24.7 2.6 %constant_dynamic-slice_fusion.3 = (f32[1,2048,128]{2,1,0:T(8,128)S(1)}, f32[1,2048,128]{2,1,0:T(8,128)}) fusion(f32[4,2048,128]{2,1,0:T(8,128)} %bitcast.65, s32[]{:T(128)S(6)} %select_n.294, s32[]{:T(128)S(6)} %select_n.296), kind=kLoop, calls=%fused_computation.61 | loop fusion | bytes 4194312 | tf_op jit(solution)/shard_map/dynamic_slice | solution.py:338
  27.3 2.6 %collective-permute-start.3 = (f32[1,2048,128]{2,1,0:T(8,128)}, f32[1,2048,128]{2,1,0:T(8,128)S(1)}, u32[]{:S(2)}, u32[]{:S(2)}) collective-permute-start(f32[1,2048,128]{2,1,0:T(8,128)} %get-tuple-element.54), channel_id=1, source_target_pairs={{0,28},{4,0},{8,4},{12,8},{16,12},{20,16},{24,20},{28,24},{1,29},{... | collective-permute-start | bytes 3145736 | tf_op jit(solution)/shard_map/ppermute | solution.py:270
  55.2 4.8 %copy.75 = bf16[32,4,8,2048]{3,2,0,1:T(8,128)(2,1)} copy(bf16[32,4,8,2048]{3,2,1,0:T(8,128)(2,1)} %bitcast.70) | data formatting | bytes 8388608 | tf_op jit(solution)/shard_map/reshape | solution.py:349
  67.4 5.6 %pad_maximum_fusion.init0.init1.init2.init3 = f32[6,2048,128]{2,1,0:T(8,128)} fusion(f32[1,2048,128]{2,1,0:T(8,128)S(1)} %collective-permute-done.3, f32[1,2048,128]{2,1,0:T(8,128)} %collective-permute-done.2, f32[4,2048,128]{2,1,0:T(8,128)} %bitcast.66), kind=kLoop, calls=%fused_computation.2 | loop fusion | flops 3145728 | bytes 12582912 | tf_op jit(solution)/shard_map/concatenate | solution.py:358
  73.0 66.1 %all-to-all-done = bf16[4,256,2688]{2,1,0:T(8,128)(2,1)} async-done(((bf16[4,256,2688]{2,1,0:T(8,128)(2,1)}), bf16[4,256,2688]{2,1,0:T(8,128)(2,1)}, u32[]{:S(2)}, u32[]{:S(2)}) %all-to-all-start) | async-done | bytes 5505056 | tf_op jit(solution)/shard_map/all_to_all | solution.py:274
  139.1 1.3 broadcast_multiply_fusion
  141.4 4.9 %all-to-all-start.1 = ((bf16[4,256,2048]{2,1,0:T(8,128)(2,1)}), bf16[4,256,2048]{2,1,0:T(8,128)(2,1)}, u32[]{:S(2)}, u32[]{:S(2)}) async-start(bf16[4,256,2048]{2,1,0:T(8,128)(2,1)} %bitcast.63), calls=%async_computation.1 | async-start | bytes 8388608 | tf_op jit(solution)/shard_map/all_to_all | solution.py:274
  146.3 1.1 dynamic-slice_bitcast_fusion.3
  147.4 1.1 collective-permute-start.6
  149.2 37.4 %scan.1 = (f32[1024,2048]{1,0:T(8,128)}, f32[4,2048,128]{2,1,0:T(8,128)}) custom-call(s32[4]{0:T(128)S(1)} %compare_select_fusion.8.idx_ref, bf16[1024,2688]{1,0:T(8,128)(2,1)} %bitcast.5.x_ref.bc_ref, bf16[1024,2688]{1,0:T(8,128)(2,1)} %bitcast.5.x_ref.bc_ref, f32[2,1024,128]{2,1,0:T(8,128)S(1)} %pad.20.dt_ref, f32[2,1024,128]{2,1,0:T(8,128)S(1)} %pad.21.log_ref, ...), custom_call_target="tpu_custom_call" | custom-call | flops 40000000000 | bytes 31457280 | tf_op jit(solution)/shard_map/scan/pallas_call | solution.py:231
  186.6 1.7 dynamic-slice_convert_fusion
  188.3 2.7 %collective-permute-start.4 = (bf16[1,2048,128]{2,1,0:T(8,128)(2,1)S(1)}, bf16[1,2048,128]{2,1,0:T(8,128)(2,1)S(1)}, u32[]{:S(2)}, u32[]{:S(2)}) collective-permute-start(bf16[1,2048,128]{2,1,0:T(8,128)(2,1)S(1)} %get-tuple-element.52), channel_id=1, source_target_pairs={{0,28},{4,0},{8,4},{12,8},{16,12},{20,16},{24,20},{28,24},{1,29},{... | collective-permute-start | bytes 1572872 | tf_op jit(solution)/shard_map/ppermute | solution.py:270
  192.5 10.0 %collective-permute-done.4 = bf16[1,2048,128]{2,1,0:T(8,128)(2,1)S(1)} collective-permute-done((bf16[1,2048,128]{2,1,0:T(8,128)(2,1)S(1)}, bf16[1,2048,128]{2,1,0:T(8,128)(2,1)S(1)}, u32[]{:S(2)}, u32[]{:S(2)}) %collective-permute-start.4) | collective-permute-done | bytes 524320 | tf_op jit(solution)/shard_map/ppermute | solution.py:270
  202.4 2.0 collective-permute-done.5
  204.4 2.8 %convert_select_fusion.3 = (f32[1,2048,128]{2,1,0:T(8,128)S(1)}, f32[1,2048,128]{2,1,0:T(8,128)S(1)}, f32[1,2048,128]{2,1,0:T(8,128)S(1)}, f32[1,2048,128]{2,1,0:T(8,128)S(1)}) fusion(f32[4,2048,128]{2,1,0:T(8,128)} %get-tuple-element.11, s32[]{:T(128)S(6)} %select_n.305, bf16[1,2048,128]{2,1,0:T(8,128)(2,1)S(1)} %collective-permute-done.4, ...), kind=kLoop, calls=%fused_computation.12 | loop fusion | flops 3145728 | bytes 9437208 | tf_op jit(solution)/shard_map/jit(_where)/select_n | solution.py:418
  207.2 2.3 pad_maximum_fusion.1
  209.5 29.6 %all-to-all-done.1 = bf16[4,256,2048]{2,1,0:T(8,128)(2,1)} async-done(((bf16[4,256,2048]{2,1,0:T(8,128)(2,1)}), bf16[4,256,2048]{2,1,0:T(8,128)(2,1)}, u32[]{:S(2)}, u32[]{:S(2)}) %all-to-all-start.1) | async-done | bytes 4194336 | tf_op jit(solution)/shard_map/all_to_all | solution.py:274
  239.1 9.6 %gate.1 = bf16[1024,2048]{1,0:T(8,128)(2,1)} custom-call(f32[1024,2048]{1,0:T(8,128)} %get-tuple-element.9.y_ref, bf16[1024,2048]{1,0:T(8,128)(2,1)} %bitcast.21.z_ref, f32[1,2048]{1,0:T(1,128)} %bitcast.84), custom_call_target="tpu_custom_call" | custom-call | flops 40000000 | bytes 16777216 | tf_op jit(solution)/shard_map/gate/pallas_call | solution.py:251
  (89 shorter events, 7.8 us)
Async XLA Ops:
  10.7 6.5 %copy-start.7 = (s32[32]{0:T(128)S(1)}, s32[32]{0:T(128)}, u32[]{:S(2)}) copy-start(s32[32]{0:T(128)} %param.30) | copy-start | bytes 388
  10.7 6.5 %copy-start.4 = (s32[32]{0:T(128)S(1)}, s32[32]{0:T(128)}, u32[]{:S(2)}) copy-start(s32[32]{0:T(128)} %param.31) | copy-start | bytes 388
  10.7 6.7 %copy-start.6 = (s32[32]{0:T(128)S(1)}, s32[32]{0:T(128)}, u32[]{:S(2)}) copy-start(s32[32]{0:T(128)} %param.29) | copy-start | bytes 388
  10.7 11.6 %copy-start.2 = (f32[4,3,2048]{2,0,1:T(4,128)S(1)}, f32[4,3,2048]{2,0,1:T(4,128)}, u32[]{:S(2)}) copy-start(f32[4,3,2048]{2,0,1:T(4,128)} %param.27) | copy-start | bytes 294916
  10.8 11.6 %copy-start.3 = (f32[4,3,512]{2,0,1:T(4,128)S(1)}, f32[4,3,512]{2,0,1:T(4,128)}, u32[]{:S(2)}) copy-start(f32[4,3,512]{2,0,1:T(4,128)} %param.28) | copy-start | bytes 73732
  10.8 20.7 %copy-start.9 = (f32[32]{0:T(128)S(1)}, f32[32]{0:T(128)}, u32[]{:S(2)}) copy-start(f32[32]{0:T(128)} %param.22) | copy-start | bytes 388
  10.8 20.7 %copy-start.1 = (f32[5,512]{1,0:T(8,128)S(1)}, f32[5,512]{1,0:T(8,128)}, u32[]{:S(2)}) copy-start(f32[5,512]{1,0:T(8,128)} %par_bc_ref.1) | copy-start | bytes 30724
  10.8 128.3 %all-to-all-start = ((bf16[4,256,2688]{2,1,0:T(8,128)(2,1)}), bf16[4,256,2688]{2,1,0:T(8,128)(2,1)}, u32[]{:S(2)}, u32[]{:S(2)}) async-start(bf16[4,256,2688]{2,1,0:T(8,128)(2,1)} %fusion.1), calls=%async_computation | async-start | bytes 11010048 | tf_op jit(solution)/shard_map/all_to_all | solution.py:274
  17.2 14.6 %copy-start = (f32[5,2048]{1,0:T(8,128)S(1)}, f32[5,2048]{1,0:T(8,128)}, u32[]{:S(2)}) copy-start(f32[5,2048]{1,0:T(8,128)} %par_x_ref.1) | copy-start | bytes 122884
  22.5 44.1 %collective-permute-start.1 = (f32[1,3,2560]{2,0,1:T(1,128)S(1)}, f32[1,3,2560]{2,0,1:T(1,128)S(1)}, u32[]{:S(2)}, u32[]{:S(2)}) collective-permute-start(f32[1,3,2560]{2,0,1:T(1,128)S(1)} %get-tuple-element.67), channel_id=1, source_target_pairs={{0,28},{4,0},{8,4},{12,8},{16,12},{20,16},{24,20},{28,24},{1,29},{... | collective-permute-start | bytes 92168 | tf_op jit(solution)/shard_map/ppermute | solution.py:270
  24.7 41.9 %collective-permute-start = (f32[1,3,2560]{2,0,1:T(1,128)S(1)}, f32[1,3,2560]{2,0,1:T(1,128)S(1)}, u32[]{:S(2)}, u32[]{:S(2)}) collective-permute-start(f32[1,3,2560]{2,0,1:T(1,128)S(1)} %get-tuple-element.66), channel_id=1, source_target_pairs={{0,4},{4,8},{8,12},{12,16},{16,20},{20,24},{24,28},{28,0},{1,5},{5... | collective-permute-start | bytes 92168 | tf_op jit(solution)/shard_map/ppermute | solution.py:270
  27.3 32.7 %copy-start.8 = (f32[32]{0:T(128)S(1)}, f32[32]{0:T(128)}, u32[]{:S(2)}) copy-start(f32[32]{0:T(128)} %param.24) | copy-start | bytes 388
  27.3 40.0 %collective-permute-start.3 = (f32[1,2048,128]{2,1,0:T(8,128)}, f32[1,2048,128]{2,1,0:T(8,128)S(1)}, u32[]{:S(2)}, u32[]{:S(2)}) collective-permute-start(f32[1,2048,128]{2,1,0:T(8,128)} %get-tuple-element.54), channel_id=1, source_target_pairs={{0,28},{4,0},{8,4},{12,8},{16,12},{20,16},{24,20},{28,24},{1,29},{... | collective-permute-start | bytes 3145736 | tf_op jit(solution)/shard_map/ppermute | solution.py:270
  30.0 37.4 %collective-permute-start.2 = (f32[1,2048,128]{2,1,0:T(8,128)S(1)}, f32[1,2048,128]{2,1,0:T(8,128)}, u32[]{:S(2)}, u32[]{:S(2)}) collective-permute-start(f32[1,2048,128]{2,1,0:T(8,128)S(1)} %get-tuple-element.53), channel_id=1, source_target_pairs={{0,4},{4,8},{8,12},{12,16},{16,20},{20,24},{24,28},{28,0},{1,5},{5... | collective-permute-start | bytes 3145736 | tf_op jit(solution)/shard_map/ppermute | solution.py:270
  67.3 71.7 %copy-start.5 = (f32[32]{0:T(128)S(1)}, f32[32]{0:T(128)}, u32[]{:S(2)}) copy-start(f32[32]{0:T(128)} %param.23) | copy-start | bytes 388
  141.4 97.7 %all-to-all-start.1 = ((bf16[4,256,2048]{2,1,0:T(8,128)(2,1)}), bf16[4,256,2048]{2,1,0:T(8,128)(2,1)}, u32[]{:S(2)}, u32[]{:S(2)}) async-start(bf16[4,256,2048]{2,1,0:T(8,128)(2,1)} %bitcast.63), calls=%async_computation.1 | async-start | bytes 8388608 | tf_op jit(solution)/shard_map/all_to_all | solution.py:274
  147.4 43.5 %collective-permute-start.6 = (bf16[1,3,2560]{2,1,0:T(4,128)(2,1)S(1)}, bf16[1,3,2560]{2,1,0:T(4,128)(2,1)S(1)}, u32[]{:S(2)}, u32[]{:S(2)}) collective-permute-start(bf16[1,3,2560]{2,1,0:T(4,128)(2,1)S(1)} %get-tuple-element.69), channel_id=1, source_target_pairs={{0,28},{4,0},{8,4},{12,8},{16,12},{20,16},{24,20},{28,24},{1,29},{... | collective-permute-start | bytes 46088 | tf_op jit(solution)/shard_map/ppermute | solution.py:270
  148.6 42.4 %collective-permute-start.7 = (bf16[1,3,2560]{2,1,0:T(4,128)(2,1)S(1)}, bf16[1,3,2560]{2,1,0:T(4,128)(2,1)S(1)}, u32[]{:S(2)}, u32[]{:S(2)}) collective-permute-start(bf16[1,3,2560]{2,1,0:T(4,128)(2,1)S(1)} %get-tuple-element.68), channel_id=1, source_target_pairs={{0,4},{4,8},{8,12},{12,16},{16,20},{20,24},{24,28},{28,0},{1,5},{5... | collective-permute-start | bytes 46088 | tf_op jit(solution)/shard_map/ppermute | solution.py:270
  188.3 14.2 %collective-permute-start.4 = (bf16[1,2048,128]{2,1,0:T(8,128)(2,1)S(1)}, bf16[1,2048,128]{2,1,0:T(8,128)(2,1)S(1)}, u32[]{:S(2)}, u32[]{:S(2)}) collective-permute-start(bf16[1,2048,128]{2,1,0:T(8,128)(2,1)S(1)} %get-tuple-element.52), channel_id=1, source_target_pairs={{0,28},{4,0},{8,4},{12,8},{16,12},{20,16},{24,20},{28,24},{1,29},{... | collective-permute-start | bytes 1572872 | tf_op jit(solution)/shard_map/ppermute | solution.py:270
  191.0 13.5 %collective-permute-start.5 = (bf16[1,2048,128]{2,1,0:T(8,128)(2,1)S(1)}, bf16[1,2048,128]{2,1,0:T(8,128)(2,1)S(1)}, u32[]{:S(2)}, u32[]{:S(2)}) collective-permute-start(bf16[1,2048,128]{2,1,0:T(8,128)(2,1)S(1)} %get-tuple-element.51), channel_id=1, source_target_pairs={{0,4},{4,8},{8,12},{12,16},{16,20},{20,24},{24,28},{28,0},{1,5},{5... | collective-permute-start | bytes 1572872 | tf_op jit(solution)/shard_map/ppermute | solution.py:270
